TPU v7x, 32 devices: a whole 2x2x4 slice. The times are simulated.
32 devices in a mesh: row: 8 (over y, x, core), rep: 4 (over z).
Axes of the slice: x: 2, y: 2, z: 4, core: 2. Of those that a mesh axis runs over, the one named last changes fastest.
Arguments:
- features: bfloat16 [4096, 128], P('row'), may hold values from -6 to 6
- tiles: bfloat16 [512, 4, 256, 256], P('row', 'rep'), may hold values from -0.375 to 0.375
- tile_where: int32 [512, 4, 2], P('row', 'rep'), may hold values from 0 to 15, as said below
- tile_count: int32 [8, 4], P('row', 'rep'), may hold values from 1 to 64, as said below
- degree: int32 [4096], P('row'), may hold values from 1 to 8
- self_one: bfloat16 [128, 256], replicated, may hold values from -0.5 to 0.5
- neigh_one: bfloat16 [128, 256], replicated, may hold values from -0.5 to 0.5
- self_two: bfloat16 [256, 256], replicated, may hold values from -0.375 to 0.375
- neigh_two: bfloat16 [256, 256], replicated, may hold values from -0.375 to 0.375
Outputs:
- embedding: float32 [4096, 256], P('row')
Inputs may be any that keep to these rules, and one draw needn't show every extreme that they name: `tile_where`: column 0 is a tile row of 0 to 1, column 1 a tile column of 0 to 15. `tile_count`: some block row and replica has all 64 slots live in every draw.
All inputs are finite; a program needn't handle non-finite values.
Results may differ from a plain program's by a relative error of at most 0.005.
Values may be sent and summed in bfloat16 or wider, within the bound.
A program may use at most 128 MiB of HBM per device.

v0:
```python
import jax
import jax.numpy as jnp
from jax import lax
from jax.sharding import PartitionSpec as P

TILE = 256


def spread_columns(whole):
    return lax.all_gather(whole, "row", axis=0, tiled=True)


def reduce_rows(partial_value):
    return lax.psum_scatter(partial_value, "rep", scatter_dimension=0, tiled=True)


def per_device(
    features, tiles, tile_where, tile_count, degree, self_one, neigh_one, self_two, neigh_two
):
    rows = features.shape[0]
    quarter = rows // lax.axis_size("rep")
    offset = lax.axis_index("rep") * quarter
    slots = tiles.shape[0]
    per_block = rows // TILE
    tile_block = tiles.reshape(slots, TILE, TILE)
    where_block = tile_where.reshape(slots, 2)
    live = jnp.arange(slots, dtype=jnp.int32) < tile_count.reshape(())
    segment = jnp.where(live, where_block[:, 0], per_block)
    column_ids = where_block[:, 1]

    def neighbour_sum(whole, width):
        gathered = spread_columns(whole)
        blocks = gathered.reshape(-1, TILE, width)
        columns = jnp.take(blocks, column_ids, axis=0)
        products = jnp.einsum(
            "sij,sjf->sif", tile_block, columns, preferred_element_type=jnp.float32
        )
        summed = jax.ops.segment_sum(products, segment, num_segments=per_block + 1)[:per_block]
        return reduce_rows(summed.reshape(rows, width))

    feature_share = lax.dynamic_slice_in_dim(features, offset, quarter, 0)
    width_in = features.shape[1]
    width_hidden = self_one.shape[1]
    scale = lax.dynamic_slice_in_dim(degree, offset, quarter, 0).astype(jnp.float32)[:, None]
    agg_one = (neighbour_sum(features, width_in) / scale).astype(jnp.bfloat16)
    first = jnp.dot(feature_share, self_one, preferred_element_type=jnp.float32) + jnp.dot(
        agg_one, neigh_one, preferred_element_type=jnp.float32
    )
    hidden_share = jax.nn.relu(first).astype(jnp.bfloat16)
    hidden = lax.all_gather(hidden_share, "rep", axis=0, tiled=True)
    agg_two = (neighbour_sum(hidden, width_hidden) / scale).astype(jnp.bfloat16)
    result_share = jnp.dot(hidden_share, self_two, preferred_element_type=jnp.float32) + jnp.dot(
        agg_two, neigh_two, preferred_element_type=jnp.float32
    )
    return lax.all_gather(result_share, "rep", axis=0, tiled=True)


def solution(mesh):
    return jax.shard_map(
        per_device,
        mesh=mesh,
        in_specs=(
            P("row", None),
            P("row", "rep", None, None),
            P("row", "rep", None),
            P("row", "rep"),
            P("row"),
            P(),
            P(),
            P(),
            P(),
        ),
        out_specs=P("row", None),
        check_vma=False,
    )
```

profile of v0, /device:TPU:0, one launch (start us, length us, event | category | flops | bytes accessed | tf_op | source)
XLA Modules:
  0.0 247.6 jit_solution(11848972710260489823)
XLA Ops:
  6.5 0.0 copy-start
  6.5 0.0 all-gather.3.cloned.1.call-start
  6.5 0.7 all-gather.3.cloned.1.call-update
  7.3 0.0 reduce-scatter.3.cloned.1.call-start
  8.0 0.8 fusion.24
  8.7 0.7 and_bitcast_fusion
  9.4 26.1 %all-gather.3.cloned.1.call-done = bf16[4096,128]{1,0:T(8,128)(2,1)} async-done(((bf16[512,128]{1,0:T(8,128)(2,1)}), bf16[4096,128]{1,0:T(8,128)(2,1)}) %all-gather.3.cloned.1.call-update) | async-done | bytes 1048592 | tf_op jit(solution)/shard_map/all_gather | solution.py:10
  35.5 4.3 %gather_fusion = bf16[64,256,128]{2,1,0:T(8,128)(2,1)} fusion(bf16[16,256,128]{2,1,0:T(8,128)(2,1)} %bitcast.30, s32[1024]{0:T(1024)S(1)} %pad_clamp_fusion), kind=kCustom, calls=%fused_computation | custom fusion | bytes 8388864 | tf_op jit(solution)/shard_map/jit(_take)/gather | solution.py:34
  39.7 12.6 %fusion.8 = f32[64,256,128]{1,2,0:T(8,128)} fusion(bf16[64,1,256,256]{3,2,1,0:T(8,128)(2,1)} %param.10, bf16[64,256,128]{2,1,0:T(8,128)(2,1)} %gather_fusion, pred[64]{0:T(512)(128)(4,1)S(1)} %and_bitcast_fusion), kind=kOutput, calls=%fused_computation.13 | convolution fusion | flops 1075838976 | bytes 20971584 | tf_op jit(solution)/shard_map/sij,sjf->sif/dot_general | solution.py:35
  52.3 9.0 %copy.13 = f32[64,256,128]{2,1,0:T(8,128)} copy(f32[64,256,128]{1,2,0:T(8,128)} %fusion.8) | data formatting | bytes 16777216 | tf_op jit(solution)/shard_map/sij,sjf->sif/dot_general | solution.py:35
  61.3 0.0 copy-start.1
  61.3 0.0 copy-start.3
  61.3 12.3 %scatter_fusion = f32[3,256,128]{2,1,0:T(8,128)S(1)} fusion(f32[3,256,128]{2,1,0:T(8,128)S(1)} %broadcast_in_dim.33, s32[64]{0:T(128)S(1)} %get-tuple-element.6, f32[64,256,128]{2,1,0:T(8,128)} %copy.13), kind=kCustom, calls=%fused_computation.2 | custom fusion | flops 2097152 | bytes 25166080 | tf_op jit(solution)/shard_map/scatter-add | solution.py:38
  73.6 0.7 slice.20
  74.3 0.0 reduce-scatter.3.cloned.1.call-update
  74.4 0.0 all-gather.5.cloned.1.call-start
  74.4 0.8 dynamic-slice_convert_fusion
  75.2 0.0 copy-done.1
  75.2 0.9 fusion.18
  76.1 18.1 %reduce-scatter.3.cloned.1.call-done = f32[128,128]{1,0:T(8,128)} async-done(((f32[512,128]{1,0:T(8,128)}), f32[128,128]{1,0:T(8,128)}) %reduce-scatter.3.cloned.1.call-update) | async-done | bytes 65552 | tf_op jit(solution)/shard_map/reduce_scatter | solution.py:14
  94.2 0.0 copy-done.3
  94.2 1.1 fusion.15
  95.2 14.5 %all_gather.13 = bf16[512,256]{1,0:T(8,128)(2,1)} all-gather(bf16[128,256]{1,0:T(8,128)(2,1)S(1)} %fusion.15), channel_id=1, replica_groups=mesh['row'=8,'rep'=4] {'rep'}, dimensions={0}, use_global_device_ids=true | all-gather | bytes 327680 | tf_op jit(solution)/shard_map/all_gather | solution.py:50
  109.8 0.0 all-gather.5.cloned.1.call-update
  109.8 0.0 reduce-scatter.5.cloned.1.call-start
  109.8 26.3 %all-gather.5.cloned.1.call-done = bf16[4096,256]{1,0:T(8,128)(2,1)} async-done(((bf16[512,256]{1,0:T(8,128)(2,1)}), bf16[4096,256]{1,0:T(8,128)(2,1)}) %all-gather.5.cloned.1.call-update) | async-done | bytes 2097168 | tf_op jit(solution)/shard_map/all_gather | solution.py:10
  136.2 7.1 %gather_fusion.1 = bf16[64,256,256]{2,1,0:T(8,128)(2,1)} fusion(bf16[16,256,256]{2,1,0:T(8,128)(2,1)} %bitcast.29, s32[1024]{0:T(1024)S(1)} %pad_clamp_fusion), kind=kCustom, calls=%fused_computation.1 | custom fusion | bytes 16777472 | tf_op jit(solution)/shard_map/jit(_take)/gather | solution.py:34
  143.3 17.3 %convolution_bitcast_fusion = f32[64,256,256]{1,2,0:T(8,128)} fusion(bf16[64,1,256,256]{3,2,1,0:T(8,128)(2,1)} %param.10, bf16[64,256,256]{2,1,0:T(8,128)(2,1)} %gather_fusion.1, pred[64]{0:T(512)(128)(4,1)S(1)} %and_bitcast_fusion), kind=kOutput, calls=%fused_computation.4 | convolution fusion | flops 2151677952 | bytes 33554496 | tf_op jit(solution)/shard_map/sij,sjf->sif/dot_general | solution.py:35
  160.5 17.5 %copy.15 = f32[64,256,256]{2,1,0:T(8,128)} copy(f32[64,256,256]{1,2,0:T(8,128)} %convolution_bitcast_fusion) | data formatting | bytes 33554432 | tf_op jit(solution)/shard_map/sij,sjf->sif/dot_general | solution.py:35
  178.0 0.1 broadcast_in_dim.37
  178.1 0.0 copy-start.2
  178.1 22.6 %scatter_fusion.1 = f32[3,256,256]{2,1,0:T(8,128)S(1)} fusion(f32[3,256,256]{2,1,0:T(8,128)S(1)} %broadcast_in_dim.37, s32[64]{0:T(128)S(1)} %get-tuple-element.6, f32[64,256,256]{2,1,0:T(8,128)} %copy.15), kind=kCustom, calls=%fused_computation.3 | custom fusion | flops 4194304 | bytes 50331904 | tf_op jit(solution)/shard_map/scatter-add | solution.py:38
  200.7 0.8 slice.21
  201.5 0.0 reduce-scatter.5.cloned.1.call-update
  201.6 0.0 copy-done
  201.6 0.2 fusion.25
  201.7 21.6 %reduce-scatter.5.cloned.1.call-done = f32[128,256]{1,0:T(8,128)} async-done(((f32[512,256]{1,0:T(8,128)}), f32[128,256]{1,0:T(8,128)}) %reduce-scatter.5.cloned.1.call-update) | async-done | bytes 131088 | tf_op jit(solution)/shard_map/reduce_scatter | solution.py:14
  223.3 0.0 copy-done.2
  223.3 1.1 convolution_add_fusion
  224.4 15.9 %all_gather.15 = f32[512,256]{1,0:T(8,128)S(1)} all-gather(f32[128,256]{1,0:T(8,128)S(1)} %convolution_add_fusion), channel_id=1, replica_groups=mesh['row'=8,'rep'=4] {'rep'}, dimensions={0}, use_global_device_ids=true | all-gather | bytes 655360 | tf_op jit(solution)/shard_map/all_gather | solution.py:55
  240.3 0.8 copy.22
  (2 shorter events, 0.0 us)
Async XLA Ops:
  6.5 195.0 %copy-start = (bf16[256,256]{1,0:T(8,128)(2,1)S(1)}, bf16[256,256]{1,0:T(8,128)(2,1)}, u32[]{:S(2)}) copy-start(bf16[256,256]{1,0:T(8,128)(2,1)} %param.16) | copy-start | bytes 393220
  6.5 28.9 %all-gather.3.cloned.1.call-start = ((), (), s32[]{:S(2)}) async-start(), calls=%async_computation.2 | async-start | bytes 1179648 | tf_op jit(solution)/shard_map/all_gather | solution.py:10
  7.3 86.9 %reduce-scatter.3.cloned.1.call-start = ((), (), s32[]{:S(2)}) async-start(), calls=%async_computation.3 | async-start | bytes 327680 | tf_op jit(solution)/shard_map/reduce_scatter | solution.py:14
  61.3 13.9 %copy-start.1 = (bf16[128,256]{1,0:T(8,128)(2,1)S(1)}, bf16[128,256]{1,0:T(8,128)(2,1)}, u32[]{:S(2)}) copy-start(bf16[128,256]{1,0:T(8,128)(2,1)} %param.14) | copy-start | bytes 196612
  61.3 32.8 %copy-start.3 = (bf16[128,256]{1,0:T(8,128)(2,1)S(1)}, bf16[128,256]{1,0:T(8,128)(2,1)}, u32[]{:S(2)}) copy-start(bf16[128,256]{1,0:T(8,128)(2,1)} %param.15) | copy-start | bytes 196612
  74.4 61.8 %all-gather.5.cloned.1.call-start = ((), (), s32[]{:S(2)}) async-start(), calls=%async_computation.4 | async-start | bytes 2359296 | tf_op jit(solution)/shard_map/all_gather | solution.py:10
  109.8 113.5 %reduce-scatter.5.cloned.1.call-start = ((), (), s32[]{:S(2)}) async-start(), calls=%async_computation.5 | async-start | bytes 655360 | tf_op jit(solution)/shard_map/reduce_scatter | solution.py:14
  178.1 45.3 %copy-start.2 = (bf16[256,256]{1,0:T(8,128)(2,1)S(1)}, bf16[256,256]{1,0:T(8,128)(2,1)}, u32[]{:S(2)}) copy-start(bf16[256,256]{1,0:T(8,128)(2,1)} %param.17) | copy-start | bytes 393220
Sparse Core Ops, SparseCore 0:
  9.2 26.1 all-gather.2
  74.5 19.6 reduce-scatter.2
  109.9 26.2 all-gather.4
  201.7 21.5 reduce-scatter.4
where the time goes:
time: 249 us; the launch traced here: 248 us
  waiting for transfers between devices  92.8 us (37%)
  local copies, waits for them, and re-layouts  40.2 us (16%)
  other arithmetic  37.1 us (15%)
  matrix products  33.1 us (13%)
  blocking collectives  30.4 us (12%)
  between operations  13.9 us (6%)
    all_gather x2, waiting for transfers between devices, spread_columns(): return lax.all_gather(whole, 'row', axis=0, tiled=True)  52.4 us
    reduce_scatter x2, waiting for transfers between devices, reduce_rows(): lax.psum_scatter(partial_value, 'rep', scatter_dimension=0, tiled=True)  39.6 us
    scatter-add x2, other arithmetic, neighbour_sum(): jax.ops.segment_sum(products, segment, num_segments=per_block + 1)  34.9 us
    dot_general x2, matrix products, neighbour_sum(): jnp.einsum('sij,sjf->sif', tile_block, columns, preferred_element_type=jn...  29.8 us
    dot_general x2, local copies, waits for them, and re-layouts, neighbour_sum(): jnp.einsum('sij,sjf->sif', tile_block, columns, preferred_element_type=jn...  26.4 us
    all_gather x1, blocking collectives, per_device(): return lax.all_gather(result_share, 'rep', axis=0, tiled=True)  15.9 us
    all_gather x1, blocking collectives, per_device(): hidden = lax.all_gather(hidden_share, 'rep', axis=0, tiled=True)  14.5 us
    gather x2, local copies, waits for them, and re-layouts, neighbour_sum(): columns = jnp.take(blocks, column_ids, axis=0)  11.4 us
  transfers between devices with their start and end apart: 4, of which 4 were waited for; matrix products, arithmetic and copies ran while one was open for 1% of the time, Pallas kernels for 0%

commit v1 on v0

v1 whole, which is shorter than its diff:
```python
import functools

import jax
import jax.numpy as jnp
from jax import lax
from jax.experimental import pallas as pl
from jax.experimental.pallas import tpu as pltpu
from jax.sharding import PartitionSpec as P

GROUP = 4
MESH = pl.DeviceIdType.MESH
F32 = jnp.float32
BF16 = jnp.bfloat16


def kernel(
    n_row, n_rep,
    where, mask, degree, features, tiles, self_one, neigh_one, self_two, neigh_two,
    out,
    tile_v, feat_v, share_v, w_self1, w_neigh1, w_self2, w_neigh2,
    acc1, send1, recv1, hid_v, acc2, send2, recv2, out_v,
    local_sem, f_send, f_recv, p1_send, p1_recv, h_send, h_recv, p2_send, p2_recv, o_send, o_recv,
):
    slots, tile, _ = tile_v.shape
    per_block, _, width_in = features.shape
    rows = per_block * tile
    quarter = rows // n_rep
    per_tile = tile // quarter
    chips = n_row // 2
    row, rep = lax.axis_index("row"), lax.axis_index("rep")
    chip, core = lax.div(row, 2), lax.rem(row, 2)
    sibling = chip * 2 + 1 - core
    others = [lax.rem(chip + k, chips) * 2 + core for k in range(1, chips)]
    others_sib = [lax.rem(chip + k, chips) * 2 + 1 - core for k in range(1, chips)]
    reps = [lax.rem(rep + k, n_rep) for k in range(1, n_rep)]
    reps_from = [lax.rem(rep + n_rep - k, n_rep) for k in range(1, n_rep)]

    pending = []

    def local(src, dst, sem):
        copy = pltpu.make_async_copy(src, dst, local_sem.at[sem])
        copy.start()
        return copy

    tile_copy = local(tiles, tile_v, 0)
    share_copy = local(
        features.at[lax.div(rep, per_tile), pl.ds(pl.multiple_of(lax.rem(rep, per_tile) * quarter, quarter), quarter)],
        share_v, 1,
    )
    own_copy = local(features, feat_v.at[pl.ds(row * per_block, per_block)], 2)
    w_copies = [
        local(src, dst, 3 + n)
        for n, (src, dst) in enumerate(
            ((self_one, w_self1), (neigh_one, w_neigh1), (self_two, w_self2), (neigh_two, w_neigh2))
        )
    ]

    barrier = pltpu.get_barrier_semaphore()
    peers = [(r, rep) for r in others + [sibling]] + [(row, q) for q in reps]
    for peer in peers:
        pl.semaphore_signal(barrier, inc=1, device_id=peer, device_id_type=MESH)
    pl.semaphore_wait(barrier, len(peers))

    def remote(src, dst, send, recv, to):
        copy = pltpu.make_async_remote_copy(
            src_ref=src, dst_ref=dst, send_sem=send, recv_sem=recv, device_id=to, device_id_type=MESH
        )
        copy.start()
        pending.append(copy)
        return copy

    def arrived(ref, send, recv):
        pltpu.make_async_remote_copy(
            src_ref=ref, dst_ref=ref, send_sem=send, recv_sem=recv, device_id=(sibling, rep), device_id_type=MESH
        ).wait_recv()

    def feat_at(r):
        return feat_v.at[pl.ds(r * per_block, per_block)]

    for k, r in enumerate(others):
        remote(features, feat_at(row), f_send.at[k], f_recv.at[row], (r, rep))
    remote(features, feat_at(row), f_send.at[chips - 1], f_recv.at[row], (sibling, rep))
    for k, r in enumerate(others):
        arrived(feat_at(r), f_send.at[0], f_recv.at[r])
        remote(feat_at(r), feat_at(r), f_send.at[chips + k], f_recv.at[r], (sibling, rep))

    acc1[...] = jnp.zeros_like(acc1)
    share_copy.wait()
    for copy in w_copies:
        copy.wait()
    first = jnp.dot(share_v[...], w_self1[...], preferred_element_type=F32)
    counts = jnp.broadcast_to(degree[pl.ds(rep, 1), :].astype(F32), (quarter, quarter))
    eye = lax.broadcasted_iota(jnp.int32, (quarter, quarter), 0) == lax.broadcasted_iota(
        jnp.int32, (quarter, quarter), 1
    )
    scale = jnp.sum(jnp.where(eye, counts, 0.0), axis=1, keepdims=True)
    own_copy.wait()
    tile_copy.wait()
    arrived(feat_at(sibling), f_send.at[0], f_recv.at[sibling])
    for r in others_sib:
        arrived(feat_at(r), f_send.at[0], f_recv.at[r])

    def product(held, acc):
        def body(g, carry):
            lhs, rhs = [], []
            for u in range(GROUP):
                s = g * GROUP + u
                block = held[where[1, s]]
                lhs.append(tile_v[s])
                rhs.append(
                    jnp.concatenate(
                        [
                            block * jnp.full((1, block.shape[1]), mask[i, s], F32).astype(BF16)
                            for i in range(per_block)
                        ],
                        axis=1,
                    )
                )
            acc[...] += jnp.dot(
                jnp.concatenate(lhs, axis=1), jnp.concatenate(rhs, axis=0), preferred_element_type=F32
            )
            return carry

        lax.fori_loop(0, slots // GROUP, body, 0)

    def reduce_over_rep(acc, send, recv, send_sem, recv_sem, width):
        for q in range(n_rep):
            i, h = q // per_tile, q % per_tile
            send[q] = acc[h * quarter : (h + 1) * quarter, i * width : (i + 1) * width].astype(BF16)
        for k, q in enumerate(reps):
            remote(send.at[q], recv.at[k], send_sem.at[k], recv_sem.at[k], (row, q))
        total = send[rep].astype(F32)
        for k in range(n_rep - 1):
            arrived(recv.at[k], send_sem.at[k], recv_sem.at[k])
            total += recv[k].astype(F32)
        return total

    product(feat_v, acc1)
    total1 = reduce_over_rep(acc1, send1, recv1, p1_send, p1_recv, width_in)
    agg1 = (total1 / scale).astype(BF16)
    first += jnp.dot(agg1, w_neigh1[...], preferred_element_type=F32)
    hidden = jnp.maximum(first, 0.0).astype(BF16)

    def share_at(r, q):
        start = pl.multiple_of(lax.rem(q, per_tile) * quarter, quarter)
        return hid_v.at[r * per_block + lax.div(q, per_tile), pl.ds(start, quarter)]

    share_at(row, rep)[...] = hidden
    for k, q in enumerate(reps):
        remote(share_at(row, rep), share_at(row, rep), h_send.at[0, k], h_recv.at[row, rep], (row, q))
    for n, q in enumerate([rep] + reps_from):
        if n:
            arrived(share_at(row, q), h_send.at[0, 0], h_recv.at[row, q])
        for k, r in enumerate(others):
            remote(share_at(row, q), share_at(row, q), h_send.at[1 + n, k], h_recv.at[row, q], (r, rep))
        remote(share_at(row, q), share_at(row, q), h_send.at[1 + n, chips - 1], h_recv.at[row, q], (sibling, rep))
    acc2[...] = jnp.zeros_like(acc2)
    result = jnp.dot(hidden, w_self2[...], preferred_element_type=F32)
    for n, q in enumerate([rep] + reps_from):
        for k, r in enumerate(others):
            arrived(share_at(r, q), h_send.at[0, 0], h_recv.at[r, q])
            remote(share_at(r, q), share_at(r, q), h_send.at[1 + n, chips + k], h_recv.at[r, q], (sibling, rep))
    for n, q in enumerate([rep] + reps_from):
        for r in [sibling] + others_sib:
            arrived(share_at(r, q), h_send.at[0, 0], h_recv.at[r, q])

    product(hid_v, acc2)
    total2 = reduce_over_rep(acc2, send2, recv2, p2_send, p2_recv, hid_v.shape[2])
    agg2 = (total2 / scale).astype(BF16)
    result += jnp.dot(agg2, w_neigh2[...], preferred_element_type=F32)
    out_v[rep] = result.astype(BF16)
    for k, q in enumerate(reps):
        remote(out_v.at[rep], out_v.at[rep], o_send.at[k], o_recv.at[rep], (row, q))
    for q in reps_from:
        arrived(out_v.at[q], o_send.at[0], o_recv.at[q])
    for q in range(n_rep):
        out[q * quarter : (q + 1) * quarter, :] = out_v[q]
    for copy in pending:
        copy.wait_send()


def per_device(
    features, tiles, tile_where, tile_count, degree, self_one, neigh_one, self_two, neigh_two
):
    n_row, n_rep = lax.axis_size("row"), lax.axis_size("rep")
    rows, width_in = features.shape
    slots, _, tile, _ = tiles.shape
    hid, width_out = self_two.shape
    per_block = rows // tile
    quarter = rows // n_rep
    chips = n_row // 2
    live = jnp.arange(slots, dtype=jnp.int32) < tile_count.reshape(())
    where = tile_where.reshape(slots, 2)
    rows_of = jnp.where(live, where[:, 0], per_block)
    mask = (rows_of == jnp.arange(per_block, dtype=jnp.int32)[:, None]).astype(F32)
    dma = pltpu.SemaphoreType.DMA
    any_spec = pl.BlockSpec(memory_space=pl.ANY)
    vmem = pl.BlockSpec(memory_space=pltpu.VMEM)
    out = pl.pallas_call(
        functools.partial(kernel, n_row, n_rep),
        out_shape=jax.ShapeDtypeStruct((rows, width_out), BF16),
        in_specs=[pl.BlockSpec(memory_space=pltpu.SMEM)] * 2 + [vmem] + [any_spec] * 6,
        out_specs=vmem,
        scratch_shapes=[
            pltpu.VMEM((slots, tile, tile), BF16),
            pltpu.VMEM((n_row * per_block, tile, width_in), BF16),
            pltpu.VMEM((quarter, width_in), BF16),
            pltpu.VMEM(self_one.shape, BF16),
            pltpu.VMEM(neigh_one.shape, BF16),
            pltpu.VMEM(self_two.shape, BF16),
            pltpu.VMEM(neigh_two.shape, BF16),
            pltpu.VMEM((tile, per_block * width_in), F32),
            pltpu.VMEM((n_rep, quarter, width_in), BF16),
            pltpu.VMEM((n_rep - 1, quarter, width_in), BF16),
            pltpu.VMEM((n_row * per_block, tile, hid), BF16),
            pltpu.VMEM((tile, per_block * hid), F32),
            pltpu.VMEM((n_rep, quarter, hid), BF16),
            pltpu.VMEM((n_rep - 1, quarter, hid), BF16),
            pltpu.VMEM((n_rep, quarter, width_out), BF16),
            dma((7,)),
            dma((2 * chips,)),
            dma((n_row,)),
            dma((n_rep - 1,)),
            dma((n_rep - 1,)),
            dma((1 + n_rep, max(2 * chips, n_rep))),
            dma((n_row, n_rep)),
            dma((n_rep - 1,)),
            dma((n_rep - 1,)),
            dma((n_rep - 1,)),
            dma((n_rep,)),
        ],
        compiler_params=pltpu.CompilerParams(
            collective_id=0, has_side_effects=True, vmem_limit_bytes=56 * 1024 * 1024
        ),
        name="sage",
    )(
        where.T, mask, degree.reshape(n_rep, quarter), features.reshape(per_block, tile, width_in), tiles.reshape(slots, tile, tile),
        self_one, neigh_one, self_two, neigh_two,
    )
    return out.astype(F32)


def solution(mesh):
    return jax.shard_map(
        per_device,
        mesh=mesh,
        in_specs=(
            P("row", None),
            P("row", "rep", None, None),
            P("row", "rep", None),
            P("row", "rep"),
            P("row"),
            P(),
            P(),
            P(),
            P(),
        ),
        out_specs=P("row", None),
        check_vma=False,
    )
```

time: 249 us -> 66.1 us (0.27)
  waiting for transfers between devices: 92.8 us -> 0 us
  Pallas kernels: 0 us -> 62.3 us
  local copies, waits for them, and re-layouts: 40.2 us -> 0 us
  other arithmetic: 37.1 us -> 3.03 us
  matrix products: 33.1 us -> 0 us
  blocking collectives: 30.4 us -> 0 us
  between operations: 13.9 us -> 0.66 us
    pallas_call x0 -> x1, Pallas kernels: none -> 62.3 us  [per_device(): pl.pallas_call(functools.partial(kernel, n_row, n_rep), out_shape=jax.Sha...]
    all_gather x2 -> x0, waiting for transfers between devices: 52.4 us -> none  [spread_columns(): return lax.all_gather(whole, 'row', axis=0, tiled=True)]
    reduce_scatter x2 -> x0, waiting for transfers between devices: 39.6 us -> none  [reduce_rows(): lax.psum_scatter(partial_value, 'rep', scatter_dimension=0, tiled=True)]
    scatter-add x2 -> x0, other arithmetic: 34.9 us -> none  [neighbour_sum(): jax.ops.segment_sum(products, segment, num_segments=per_block + 1)]
    dot_general x6 -> x0, matrix products: 33.1 us -> none  [the longest x2 29.8 us: neighbour_sum(): jnp.einsum('sij,sjf->sif', tile_block, columns, preferred_element_type=jn...]
    all_gather x2 -> x0, blocking collectives: 30.4 us -> none  [the longest x1 15.9 us: per_device(): return lax.all_gather(result_share, 'rep', axis=0, tiled=True)]
    dot_general x2 -> x0, local copies, waits for them, and re-layouts: 26.4 us -> none  [neighbour_sum(): jnp.einsum('sij,sjf->sif', tile_block, columns, preferred_element_type=jn...]
    gather x2 -> x0, local copies, waits for them, and re-layouts: 11.4 us -> none  [neighbour_sum(): columns = jnp.take(blocks, column_ids, axis=0)]
  transfers between devices with their start and end apart: 4 -> 0, of which waited for: 4 -> 0; matrix products, arithmetic and copies ran while one was open for 1% -> 0% of each run, Pallas kernels for 0% -> 0%
where the time goes in v1:
time: 66.1 us; the launch traced here: 65.9 us
  Pallas kernels  62.3 us (94%)
  other arithmetic  3.03 us (5%)
    pallas_call x1, Pallas kernels, per_device(): pl.pallas_call(functools.partial(kernel, n_row, n_rep), out_shape=jax.Sha...  62.3 us
    convert_element_type x1, other arithmetic, per_device(): return out.astype(F32)  1.78 us

profile of v1, /device:TPU:0, one launch (start us, length us, event | category | flops | bytes accessed | tf_op | source)
XLA Modules:
  0.0 65.9 jit_solution(11566003004120278378)
XLA Ops:
  0.7 0.7 %compare_select_fusion = s32[64]{0:T(128)S(1)} fusion(s32[64,2]{0,1:T(2,128)} %bitcast.13, s32[]{:T(128)} %bitcast.9), kind=kLoop, calls=%fused_computation.1 | loop fusion | flops 128 | bytes 516 | tf_op jit(solution)/shard_map/jit(_where)/select_n | solution.py:194
  1.3 0.6 compare_convert_fusion.mask
  1.9 62.3 %sage.1 = bf16[512,256]{1,0:T(8,128)(2,1)} custom-call(s32[2,64]{1,0:T(2,128)} %bitcast.14, f32[2,64]{1,0:T(2,128)} %compare_convert_fusion.mask, s32[4,128]{1,0:T(4,128)} %bitcast.12, bf16[2,256,128]{2,1,0:T(8,128)(2,1)} %bitcast.11, bf16[64,256,256]{2,1,0:T(8,128)(2,1)} %bitcast.10, bf16[128,256]{1,0:T(8,128)(2,1)} %self_one.1, ...), custom_call_target="tpu_custom_call" | custom-call | tf_op jit(solution)/shard_map/sage/pallas_call | solution.py:199
  64.2 1.8 %convert_element_type.7 = f32[512,256]{1,0:T(8,128)} convert(bf16[512,256]{1,0:T(8,128)(2,1)} %sage.1) | non-fusion elementwise | flops 131072 | bytes 786432 | tf_op jit(solution)/shard_map/convert_element_type | solution.py:240

commit v2 on v1

v2 whole, which is shorter than its diff:
```python
import functools

import jax
import jax.numpy as jnp
from jax import lax
from jax.experimental import pallas as pl
from jax.experimental.pallas import tpu as pltpu
from jax.sharding import PartitionSpec as P

GROUP = 8
MESH = pl.DeviceIdType.MESH
F32 = jnp.float32
BF16 = jnp.bfloat16


def kernel(
    n_row, n_rep,
    where, count, degree, features, tiles, self_one, neigh_one, self_two, neigh_two,
    out,
    tile_v, feat_v, w_one, w_self2, w_neigh2,
    acc, send1, recv1, agg_v, hid_v, send2, recv2, out_v,
    local_sem, f_send, f_recv, p1_send, p1_recv, h_send, h_recv, p2_send, p2_recv, o_send, o_recv,
):
    slots, tile, _ = tile_v.shape
    per_block, _, width_in = features.shape
    rows = per_block * tile
    quarter = rows // n_rep
    per_tile = tile // quarter
    chips = n_row // 2
    row, rep = lax.axis_index("row"), lax.axis_index("rep")
    chip, core = lax.div(row, 2), lax.rem(row, 2)
    sibling = chip * 2 + 1 - core
    others = [lax.rem(chip + k, chips) * 2 + core for k in range(1, chips)]
    others_sib = [lax.rem(chip + k, chips) * 2 + 1 - core for k in range(1, chips)]
    reps = [lax.rem(rep + k, n_rep) for k in range(1, n_rep)]
    reps_from = [lax.rem(rep + n_rep - k, n_rep) for k in range(1, n_rep)]

    pending = []

    def local(src, dst, sem):
        copy = pltpu.make_async_copy(src, dst, local_sem.at[sem])
        copy.start()
        return copy

    tile_copy = local(tiles, tile_v, 0)
    own_copy = local(features, feat_v.at[pl.ds(row * per_block, per_block)], 2)
    w_copies = [
        local(src, dst, 3 + n)
        for n, (src, dst) in enumerate(
            (
                (self_one, w_one.at[pl.ds(0, width_in)]),
                (neigh_one, w_one.at[pl.ds(width_in, width_in)]),
                (self_two, w_self2),
                (neigh_two, w_neigh2),
            )
        )
    ]

    barrier = pltpu.get_barrier_semaphore()
    peers = [(r, rep) for r in others + [sibling]] + [(row, q) for q in reps]
    for peer in peers:
        pl.semaphore_signal(barrier, inc=1, device_id=peer, device_id_type=MESH)
    pl.semaphore_wait(barrier, len(peers))

    def remote(src, dst, send, recv, to):
        copy = pltpu.make_async_remote_copy(
            src_ref=src, dst_ref=dst, send_sem=send, recv_sem=recv, device_id=to, device_id_type=MESH
        )
        copy.start()
        pending.append(copy)
        return copy

    def arrived(ref, send, recv):
        pltpu.make_async_remote_copy(
            src_ref=ref, dst_ref=ref, send_sem=send, recv_sem=recv, device_id=(sibling, rep), device_id_type=MESH
        ).wait_recv()

    def feat_at(r):
        return feat_v.at[pl.ds(r * per_block, per_block)]

    for k, r in enumerate(others):
        remote(features, feat_at(row), f_send.at[k], f_recv.at[row], (r, rep))
    remote(features, feat_at(row), f_send.at[chips - 1], f_recv.at[row], (sibling, rep))
    for k, r in enumerate(others):
        arrived(feat_at(r), f_send.at[0], f_recv.at[r])
        remote(feat_at(r), feat_at(r), f_send.at[chips + k], f_recv.at[r], (sibling, rep))

    counts = jnp.broadcast_to(degree[pl.ds(rep, 1), :].astype(F32), (quarter, quarter))
    eye = lax.broadcasted_iota(jnp.int32, (quarter, quarter), 0) == lax.broadcasted_iota(
        jnp.int32, (quarter, quarter), 1
    )
    scale = jnp.sum(jnp.where(eye, counts, 0.0), axis=1, keepdims=True)
    own_copy.wait()
    tile_copy.wait()
    arrived(feat_at(sibling), f_send.at[0], f_recv.at[sibling])
    for r in others_sib:
        arrived(feat_at(r), f_send.at[0], f_recv.at[r])

    def product(held, start, width):
        acc[...] = jnp.zeros_like(acc)
        live_slots = jnp.full((1, width), count[0, 0], jnp.int32)

        def body(g, carry):
            lhs, rhs = [], []
            for u in range(GROUP):
                s = g * GROUP + u
                block = held[where[1, s], :, start : start + width]
                tile_row = jnp.full((1, width), where[0, s], jnp.int32)
                live = jnp.full((1, width), s, jnp.int32) < live_slots
                lhs.append(tile_v[s])
                rhs.append(
                    jnp.concatenate(
                        [
                            block * jnp.where(live & (tile_row == i), 1.0, 0.0).astype(BF16)
                            for i in range(per_block)
                        ],
                        axis=1,
                    )
                )
            acc[...] += jnp.dot(
                jnp.concatenate(lhs, axis=1), jnp.concatenate(rhs, axis=0), preferred_element_type=F32
            )
            return carry

        lax.fori_loop(0, slots // GROUP, body, 0)

    def send_partials(send, recv, send_sem, recv_sem, width):
        for q in range(n_rep):
            i, h = q // per_tile, q % per_tile
            part = acc[h * quarter : (h + 1) * quarter, i * width : (i + 1) * width]
            send[q] = part.astype(send.dtype)
        for k, q in enumerate(reps):
            remote(send.at[q], recv.at[k], send_sem.at[k], recv_sem.at[k], (row, q))

    def sum_partials(send, recv, send_sem, recv_sem):
        total = send[rep].astype(F32)
        for k in range(n_rep - 1):
            arrived(recv.at[k], send_sem.at[k], recv_sem.at[k])
            total += recv[k].astype(F32)
        return total

    def share_at(ref, r, q):
        start = pl.multiple_of(lax.rem(q, per_tile) * quarter, quarter)
        return ref.at[r * per_block + lax.div(q, per_tile), pl.ds(start, quarter)]

    product(feat_v, 0, width_in)
    send_partials(send1, recv1, p1_send, p1_recv, width_in)
    for copy in w_copies:
        copy.wait()
    total1 = sum_partials(send1, recv1, p1_send, p1_recv)
    share_at(agg_v, row, rep)[...] = (total1 / scale).astype(BF16)

    order = [rep] + reps_from
    for k, q in enumerate(reps):
        own = share_at(agg_v, row, rep)
        remote(own, own, h_send.at[0, k], h_recv.at[row, rep], (row, q))
    for n, q in enumerate(order):
        share = share_at(agg_v, row, q)
        if n:
            arrived(share, h_send.at[0, 0], h_recv.at[row, q])
        for k, r in enumerate(others):
            remote(share, share, h_send.at[1 + n, k], h_recv.at[row, q], (r, rep))
        remote(share, share, h_send.at[1 + n, chips - 1], h_recv.at[row, q], (sibling, rep))

    def hidden_of(r):
        for b in range(per_block):
            both = jnp.concatenate([feat_v[r * per_block + b], agg_v[r * per_block + b]], axis=1)
            first = jnp.dot(both, w_one[...], preferred_element_type=F32)
            hid_v[r * per_block + b] = jnp.maximum(first, 0.0).astype(BF16)

    hidden_of(row)
    for n, q in enumerate(order):
        for k, r in enumerate(others):
            share = share_at(agg_v, r, q)
            arrived(share, h_send.at[0, 0], h_recv.at[r, q])
            remote(share, share, h_send.at[1 + n, chips + k], h_recv.at[r, q], (sibling, rep))
    for r in others:
        hidden_of(r)
    for r in [sibling] + others_sib:
        for q in order:
            arrived(share_at(agg_v, r, q), h_send.at[0, 0], h_recv.at[r, q])
        hidden_of(r)

    parts = hid_v.shape[2] // width_in
    for c in range(parts):
        product(hid_v, c * width_in, width_in)
        send_partials(send2.at[c], recv2.at[c], p2_send.at[c], p2_recv.at[c], width_in)
    result = jnp.dot(share_at(hid_v, row, rep)[...], w_self2[...], preferred_element_type=F32)
    for c in range(parts):
        total2 = sum_partials(send2.at[c], recv2.at[c], p2_send.at[c], p2_recv.at[c])
        agg2 = (total2 / scale).astype(BF16)
        result += jnp.dot(
            agg2, w_neigh2[c * width_in : (c + 1) * width_in, :], preferred_element_type=F32
        )
    out_v[rep] = result.astype(BF16)
    for k, q in enumerate(reps):
        remote(out_v.at[rep], out_v.at[rep], o_send.at[k], o_recv.at[rep], (row, q))
    for q in reps_from:
        arrived(out_v.at[q], o_send.at[0], o_recv.at[q])
    for q in range(n_rep):
        out[q * quarter : (q + 1) * quarter, :] = out_v[q]
    for copy in pending:
        copy.wait_send()


def per_device(
    features, tiles, tile_where, tile_count, degree, self_one, neigh_one, self_two, neigh_two
):
    n_row, n_rep = lax.axis_size("row"), lax.axis_size("rep")
    rows, width_in = features.shape
    slots, _, tile, _ = tiles.shape
    hid, width_out = self_two.shape
    per_block = rows // tile
    quarter = rows // n_rep
    chips = n_row // 2
    parts = hid // width_in
    dma = pltpu.SemaphoreType.DMA
    any_spec = pl.BlockSpec(memory_space=pl.ANY)
    vmem = pl.BlockSpec(memory_space=pltpu.VMEM)
    out = pl.pallas_call(
        functools.partial(kernel, n_row, n_rep),
        out_shape=jax.ShapeDtypeStruct((rows, width_out), BF16),
        in_specs=[pl.BlockSpec(memory_space=pltpu.SMEM)] * 2 + [vmem] + [any_spec] * 6,
        out_specs=vmem,
        scratch_shapes=[
            pltpu.VMEM((slots, tile, tile), BF16),
            pltpu.VMEM((n_row * per_block, tile, width_in), BF16),
            pltpu.VMEM((2 * width_in, hid), BF16),
            pltpu.VMEM(self_two.shape, BF16),
            pltpu.VMEM(neigh_two.shape, BF16),
            pltpu.VMEM((tile, per_block * width_in), F32),
            pltpu.VMEM((n_rep, quarter, width_in), F32),
            pltpu.VMEM((n_rep - 1, quarter, width_in), F32),
            pltpu.VMEM((n_row * per_block, tile, width_in), BF16),
            pltpu.VMEM((n_row * per_block, tile, hid), BF16),
            pltpu.VMEM((parts, n_rep, quarter, width_in), BF16),
            pltpu.VMEM((parts, n_rep - 1, quarter, width_in), BF16),
            pltpu.VMEM((n_rep, quarter, width_out), BF16),
            dma((7,)),
            dma((2 * chips,)),
            dma((n_row,)),
            dma((n_rep - 1,)),
            dma((n_rep - 1,)),
            dma((1 + n_rep, max(2 * chips, n_rep))),
            dma((n_row, n_rep)),
            dma((parts, n_rep - 1)),
            dma((parts, n_rep - 1)),
            dma((n_rep - 1,)),
            dma((n_rep,)),
        ],
        compiler_params=pltpu.CompilerParams(
            collective_id=0, has_side_effects=True, vmem_limit_bytes=56 * 1024 * 1024
        ),
        name="sage",
    )(
        tile_where.reshape(slots, 2).T, tile_count, degree.reshape(n_rep, quarter), features.reshape(per_block, tile, width_in), tiles.reshape(slots, tile, tile),
        self_one, neigh_one, self_two, neigh_two,
    )
    return out.astype(F32)


def solution(mesh):
    return jax.shard_map(
        per_device,
        mesh=mesh,
        in_specs=(
            P("row", None),
            P("row", "rep", None, None),
            P("row", "rep", None),
            P("row", "rep"),
            P("row"),
            P(),
            P(),
            P(),
            P(),
        ),
        out_specs=P("row", None),
        check_vma=False,
    )
```

time: 66.1 us -> 59.3 us (0.90)
  Pallas kernels: 62.3 us -> 56.7 us
  other arithmetic: 3.03 us -> 1.78 us
    pallas_call x1, Pallas kernels: 62.3 us -> 56.7 us  [per_device(): pl.pallas_call(functools.partial(kernel, n_row, n_rep), out_shape=jax.Sha...]
    select_n x1 -> x0, other arithmetic: 0.68 us -> none  [per_device(): rows_of = jnp.where(live, where[:, 0], per_block)]
where the time goes in v2:
time: 59.3 us; the launch traced here: 59.1 us
  Pallas kernels  56.7 us (96%)
  other arithmetic  1.78 us (3%)
  between operations  0.66 us (1%)
    pallas_call x1, Pallas kernels, per_device(): pl.pallas_call(functools.partial(kernel, n_row, n_rep), out_shape=jax.Sha...  56.7 us
    convert_element_type x1, other arithmetic, per_device(): return out.astype(F32)  1.78 us

profile of v2, /device:TPU:0, one launch (start us, length us, event | category | flops | bytes accessed | tf_op | source)
XLA Modules:
  0.0 59.1 jit_solution(5827667999655970751)
XLA Ops:
  0.7 56.7 %sage.1 = bf16[512,256]{1,0:T(8,128)(2,1)} custom-call(s32[2,64]{1,0:T(2,128)} %bitcast.9, s32[1,1]{1,0:T(1,128)S(6)} %copy.10.count, s32[4,128]{1,0:T(4,128)} %bitcast.8, bf16[2,256,128]{2,1,0:T(8,128)(2,1)} %bitcast.7, bf16[64,256,256]{2,1,0:T(8,128)(2,1)} %bitcast.6, bf16[128,256]{1,0:T(8,128)(2,1)} %self_one.1, bf16[128,256]{1,0:T(8,128)(2,1)} %neigh_one.1, ...), custom_call_target="tpu_custom_call" | custom-call | tf_op jit(solution)/shard_map/sage/pallas_call | solution.py:220
  57.3 1.8 %convert_element_type.3 = f32[512,256]{1,0:T(8,128)} convert(bf16[512,256]{1,0:T(8,128)(2,1)} %sage.1) | non-fusion elementwise | flops 131072 | bytes 786432 | tf_op jit(solution)/shard_map/convert_element_type | solution.py:259

commit v3 on v2

--- a/solution.py
+++ b/solution.py
@@ -14,11 +14,11 @@
 
 
 def kernel(
-    n_row, n_rep,
-    where, count, degree, features, tiles, self_one, neigh_one, self_two, neigh_two,
+    n_row, n_rep, dense,
+    where, count, table, degree, features, tiles, self_one, neigh_one, self_two, neigh_two,
     out,
     tile_v, feat_v, w_one, w_self2, w_neigh2,
-    acc, send1, recv1, agg_v, hid_v, send2, recv2, out_v,
+    acc, send1, recv1, agg_v, hid_v, cell_v, acc2, send2, recv2, out_v,
     local_sem, f_send, f_recv, p1_send, p1_recv, h_send, h_recv, p2_send, p2_recv, o_send, o_recv,
 ):
     slots, tile, _ = tile_v.shape
@@ -75,12 +75,30 @@
             src_ref=ref, dst_ref=ref, send_sem=send, recv_sem=recv, device_id=(sibling, rep), device_id_type=MESH
         ).wait_recv()
 
+    def build_cells():
+        chunk = min(64, tile)
+        cell_v[slots] = jnp.zeros((tile, tile), BF16)
+        for start in range(0, tile, chunk):
+
+            def body(g, run):
+                for u in range(GROUP):
+                    k = g * GROUP + u
+                    piece = tile_v[table[0, k], start : start + chunk, :].astype(F32)
+                    run = run * jnp.full((1, tile), table[1, k], jnp.int32).astype(F32) + piece
+                    cell_v[k, start : start + chunk, :] = run.astype(BF16)
+                return run
+
+            lax.fori_loop(0, slots // GROUP, body, jnp.zeros((chunk, tile), F32))
+
     def feat_at(r):
         return feat_v.at[pl.ds(r * per_block, per_block)]
 
     for k, r in enumerate(others):
         remote(features, feat_at(row), f_send.at[k], f_recv.at[row], (r, rep))
     remote(features, feat_at(row), f_send.at[chips - 1], f_recv.at[row], (sibling, rep))
+    if dense:
+        tile_copy.wait()
+        build_cells()
     for k, r in enumerate(others):
         arrived(feat_at(r), f_send.at[0], f_recv.at[r])
         remote(feat_at(r), feat_at(r), f_send.at[chips + k], f_recv.at[r], (sibling, rep))
@@ -91,7 +109,8 @@
     )
     scale = jnp.sum(jnp.where(eye, counts, 0.0), axis=1, keepdims=True)
     own_copy.wait()
-    tile_copy.wait()
+    if not dense:
+        tile_copy.wait()
     arrived(feat_at(sibling), f_send.at[0], f_recv.at[sibling])
     for r in others_sib:
         arrived(feat_at(r), f_send.at[0], f_recv.at[r])
@@ -124,10 +143,13 @@
 
         lax.fori_loop(0, slots // GROUP, body, 0)
 
-    def send_partials(send, recv, send_sem, recv_sem, width):
+    def send_partials(send, recv, send_sem, recv_sem, width, start=None):
         for q in range(n_rep):
             i, h = q // per_tile, q % per_tile
-            part = acc[h * quarter : (h + 1) * quarter, i * width : (i + 1) * width]
+            if start is None:
+                part = acc[h * quarter : (h + 1) * quarter, i * width : (i + 1) * width]
+            else:
+                part = acc2[i, h * quarter : (h + 1) * quarter, start : start + width]
             send[q] = part.astype(send.dtype)
         for k, q in enumerate(reps):
             remote(send.at[q], recv.at[k], send_sem.at[k], recv_sem.at[k], (row, q))
@@ -167,7 +189,23 @@
             both = jnp.concatenate([feat_v[r * per_block + b], agg_v[r * per_block + b]], axis=1)
             first = jnp.dot(both, w_one[...], preferred_element_type=F32)
             hid_v[r * per_block + b] = jnp.maximum(first, 0.0).astype(BF16)
-
+        if dense:
+            columns = n_row * per_block
+            lhs = jnp.concatenate(
+                [
+                    jnp.concatenate(
+                        [cell_v[table[2, i * columns + r * per_block + b]] for b in range(per_block)], axis=1
+                    )
+                    for i in range(per_block)
+                ],
+                axis=0,
+            )
+            rhs = jnp.concatenate([hid_v[r * per_block + b] for b in range(per_block)], axis=0)
+            step = jnp.dot(lhs, rhs, preferred_element_type=F32)
+            for i in range(per_block):
+                acc2[i] += step[i * tile : (i + 1) * tile]
+
+    acc2[...] = jnp.zeros_like(acc2)
     hidden_of(row)
     for n, q in enumerate(order):
         for k, r in enumerate(others):
@@ -183,8 +221,11 @@
 
     parts = hid_v.shape[2] // width_in
     for c in range(parts):
-        product(hid_v, c * width_in, width_in)
-        send_partials(send2.at[c], recv2.at[c], p2_send.at[c], p2_recv.at[c], width_in)
+        if not dense:
+            product(hid_v, c * width_in, width_in)
+        send_partials(
+            send2.at[c], recv2.at[c], p2_send.at[c], p2_recv.at[c], width_in, c * width_in if dense else None
+        )
     result = jnp.dot(share_at(hid_v, row, rep)[...], w_self2[...], preferred_element_type=F32)
     for c in range(parts):
         total2 = sum_partials(send2.at[c], recv2.at[c], p2_send.at[c], p2_recv.at[c])
@@ -203,6 +244,30 @@
         copy.wait_send()
 
 
+def order_kernel(columns, cells, count, where, table):
+    slots = where.shape[1]
+
+    def total(cond, value, axis):
+        return jnp.sum(jnp.where(cond, value, 0.0), axis=axis, keepdims=True)
+
+    square = (slots, slots)
+    sub = lax.broadcasted_iota(jnp.int32, square, 0)
+    lane = lax.broadcasted_iota(jnp.int32, square, 1)
+    spread = jnp.broadcast_to(where[0:1, :] * columns + where[1:2, :], square)
+    of_lane = jnp.where(lane < jnp.full(square, count[0, 0], jnp.int32), spread, cells).astype(F32)
+    of_sub = total(lane == sub, of_lane, 1)
+    earlier = (of_lane == of_sub) & (lane < sub)
+    rank = total((of_lane < of_sub) | earlier, 1.0, 1)
+    seen = total(earlier, 1.0, 1)
+    hit = rank == lane.astype(F32)
+    table[0:1, 0:slots] = total(hit, sub.astype(F32), 0).astype(jnp.int32)
+    table[1:2, 0:slots] = total(hit & (seen > 0.0), 1.0, 0).astype(jnp.int32)
+    cell = lax.broadcasted_iota(jnp.int32, (slots, cells), 1).astype(F32)
+    upto = total(of_sub <= cell, 1.0, 0)
+    here = total(of_sub == cell, 1.0, 0)
+    table[2:3, 0:cells] = jnp.where(here > 0.0, upto - 1.0, float(slots)).astype(jnp.int32)
+
+
 def per_device(
     features, tiles, tile_where, tile_count, degree, self_one, neigh_one, self_two, neigh_two
 ):
@@ -214,13 +279,28 @@
     quarter = rows // n_rep
     chips = n_row // 2
     parts = hid // width_in
+    columns = n_row * per_block
+    cells = per_block * columns
+    dense = cells <= slots
+    where = tile_where.reshape(slots, 2).T
+    smem = pl.BlockSpec(memory_space=pltpu.SMEM)
+    if dense:
+        table = pl.pallas_call(
+            functools.partial(order_kernel, columns, cells),
+            out_shape=jax.ShapeDtypeStruct((3, max(slots, cells)), jnp.int32),
+            in_specs=[smem, pl.BlockSpec(memory_space=pltpu.VMEM)],
+            out_specs=pl.BlockSpec(memory_space=pltpu.VMEM),
+            name="order",
+        )(tile_count, where)
+    else:
+        table = where
     dma = pltpu.SemaphoreType.DMA
     any_spec = pl.BlockSpec(memory_space=pl.ANY)
     vmem = pl.BlockSpec(memory_space=pltpu.VMEM)
     out = pl.pallas_call(
-        functools.partial(kernel, n_row, n_rep),
+        functools.partial(kernel, n_row, n_rep, dense),
         out_shape=jax.ShapeDtypeStruct((rows, width_out), BF16),
-        in_specs=[pl.BlockSpec(memory_space=pltpu.SMEM)] * 2 + [vmem] + [any_spec] * 6,
+        in_specs=[smem] * 3 + [vmem] + [any_spec] * 6,
         out_specs=vmem,
         scratch_shapes=[
             pltpu.VMEM((slots, tile, tile), BF16),
@@ -233,6 +313,8 @@
             pltpu.VMEM((n_rep - 1, quarter, width_in), F32),
             pltpu.VMEM((n_row * per_block, tile, width_in), BF16),
             pltpu.VMEM((n_row * per_block, tile, hid), BF16),
+            pltpu.VMEM((slots + 1 if dense else 1, tile, tile), BF16),
+            pltpu.VMEM((per_block, tile, hid), F32),
             pltpu.VMEM((parts, n_rep, quarter, width_in), BF16),
             pltpu.VMEM((parts, n_rep - 1, quarter, width_in), BF16),
             pltpu.VMEM((n_rep, quarter, width_out), BF16),
@@ -253,7 +335,7 @@
         ),
         name="sage",
     )(
-        tile_where.reshape(slots, 2).T, tile_count, degree.reshape(n_rep, quarter), features.reshape(per_block, tile, width_in), tiles.reshape(slots, tile, tile),
+        where, tile_count, table, degree.reshape(n_rep, quarter), features.reshape(per_block, tile, width_in), tiles.reshape(slots, tile, tile),
         self_one, neigh_one, self_two, neigh_two,
     )
     return out.astype(F32)

time: 59.3 us -> 56.5 us (0.953)
  Pallas kernels: 56.7 us -> 53.9 us
    pallas_call x1 -> x2, Pallas kernels: 56.7 us -> 53.9 us  [the longest x1 52.4 us: per_device(): pl.pallas_call(functools.partial(kernel, n_row, n_rep, dense), out_shape=...]
where the time goes in v3:
time: 56.5 us; the launch traced here: 56.3 us
  Pallas kernels  53.9 us (95%)
  other arithmetic  1.78 us (3%)
  between operations  0.66 us (1%)
    pallas_call x1, Pallas kernels, per_device(): pl.pallas_call(functools.partial(kernel, n_row, n_rep, dense), out_shape=...  52.4 us
    convert_element_type x1, other arithmetic, per_device(): return out.astype(F32)  1.78 us
    pallas_call x1, Pallas kernels, per_device(): pl.pallas_call(functools.partial(order_kernel, columns, cells), out_shape...  1.45 us

profile of v3, /device:TPU:0, one launch (start us, length us, event | category | flops | bytes accessed | tf_op | source)
XLA Modules:
  0.0 56.3 jit_solution(12584135864190527456)
XLA Ops:
  0.7 1.4 %order.1.table = s32[3,64]{1,0:T(4,128)} custom-call(s32[1,1]{1,0:T(1,128)S(6)} %copy.10.count, s32[2,64]{1,0:T(2,128)} %bitcast.8), custom_call_target="tpu_custom_call" | custom-call | tf_op jit(solution)/shard_map/order/pallas_call | solution.py:288
  2.1 52.4 %sage.1 = bf16[512,256]{1,0:T(8,128)(2,1)} custom-call(s32[2,64]{1,0:T(2,128)} %bitcast.9, s32[1,1]{1,0:T(1,128)S(6)} %copy.10.count, s32[3,64]{1,0:T(4,128)} %order.1.table, s32[4,128]{1,0:T(4,128)} %bitcast.10, bf16[2,256,128]{2,1,0:T(8,128)(2,1)} %bitcast.7, bf16[64,256,256]{2,1,0:T(8,128)(2,1)} %bitcast.6, bf16[128,256]{1,0:T(8,128)(2,1)} %self_one.1, ...), custom_call_target="tpu_custom_call" | custom-call | tf_op jit(solution)/shard_map/sage/pallas_call | solution.py:300
  54.5 1.8 %convert_element_type.3 = f32[512,256]{1,0:T(8,128)} convert(bf16[512,256]{1,0:T(8,128)(2,1)} %sage.1) | non-fusion elementwise | flops 131072 | bytes 786432 | tf_op jit(solution)/shard_map/convert_element_type | solution.py:341
